TPU v7x, 32 devices: a whole 2x2x4 slice. The times are simulated.
32 devices in a mesh: dp: 4 (over z), fsdp: 4 (over y, core), query: 2 (over x).
Axes of the slice: x: 2, y: 2, z: 4, core: 2. Of those that a mesh axis runs over, the one named last changes fastest.
Arguments:
- queries: bfloat16 [4, 1024, 1024], P('fsdp', ('dp', 'query')), may hold values from -40 to 40
- passages: bfloat16 [4, 2048, 1024], P('fsdp', ('dp', 'query')), may hold values from -6 to 6
- head_weight: bfloat16 [1024, 1024], P('fsdp'), may hold values from -0.1875 to 0.1875
- positives: int32 [4, 1024], P('fsdp', ('dp', 'query')), may hold values from 0 to 2047
- negative_ids: int32 [4, 8, 2], P('fsdp', ('dp', 'query')), may hold values from 0 to 15, as said below
- negative_count: int32 [4, 8], P('fsdp', ('dp', 'query')), may hold values from 1 to 2, as said below
Outputs:
- query_loss: float32 [4, 1024], P('fsdp', ('dp', 'query'))
Inputs may be any that keep to these rules, and one draw needn't show every extreme that they name: `negative_ids`: the 2 entries of a query block are distinct passage blocks of its index shard; only the first negative_count of them are live. `negative_count`: in every aligned run of 8 query blocks one has exactly 2 live entries.
All inputs are finite; a program needn't handle non-finite values.
Results may differ from a plain program's by a relative error of at most 0.0048.
Values may be sent and summed in bfloat16 or wider, within the bound.
A program may use at most 64 MiB of HBM per device.

v0:
```python
import jax
import jax.numpy as jnp
from jax import lax
from jax.sharding import PartitionSpec as P

BLOCK = 128


masked_floor = -1e30


def joined(part, axis, combine):
    gathered = jax.tree.map(lambda a: lax.all_gather(a, axis), part)

    def take(source):
        return jax.tree.map(lambda a: lax.dynamic_index_in_dim(a, source, 0, False), gathered)

    return lax.fori_loop(
        1, lax.axis_size(axis), lambda source, state: combine(state, take(source)), take(0)
    )


def combine_stats(first, second):
    top = jnp.maximum(first[0], second[0])
    total = first[1] * jnp.exp(first[0] - top) + second[1] * jnp.exp(second[0] - top)
    return (top, total, first[2] + second[2])


def local(queries, passages, head_weight, positives, negative_ids, negative_count):
    query_rows = queries[0]
    passage_rows = passages[0]
    feature_width = query_rows.shape[1]
    scale_factor = feature_width ** (-0.5)
    query_count = query_rows.shape[0]
    shard_rows = lax.all_gather(head_weight, "fsdp", axis=0, tiled=True)
    query_sum = jnp.dot(query_rows, shard_rows, preferred_element_type=jnp.float32)
    passage_sum = jnp.dot(passage_rows, shard_rows, preferred_element_type=jnp.float32)
    query_proj = query_sum.astype(jnp.bfloat16)
    passage_proj = passage_sum.astype(jnp.bfloat16)
    paired = lax.all_gather(passage_proj, "query", axis=0, tiled=True)
    pair_count = paired.shape[0]
    pair_first = lax.axis_index("dp") * pair_count
    tile_count = pair_count // BLOCK
    tile_ids = pair_first // BLOCK + lax.iota(jnp.int32, tile_count)
    listed_ids = negative_ids[0]
    live_slot = lax.broadcasted_iota(jnp.int32, listed_ids.shape, 1) < negative_count[0][:, None]
    listed_ids = jnp.where(live_slot, listed_ids, -1)
    row_lists = jnp.repeat(listed_ids, BLOCK, axis=0)
    targets = positives[0]
    query_piece = lax.all_gather(query_proj, "dp", axis=0, tiled=True)
    list_piece = lax.all_gather(row_lists, "dp", axis=0, tiled=True)
    target_piece = lax.all_gather(targets, "dp", axis=0, tiled=True)
    local_target = target_piece - pair_first
    has_target = (local_target >= 0) & (local_target < pair_count)
    target_rows = jnp.take(paired, jnp.clip(local_target, 0, pair_count - 1), axis=0)
    target_logit = (
        jnp.sum(query_piece.astype(jnp.float32) * target_rows.astype(jnp.float32), axis=1)
        * scale_factor
    )
    target_listed = jnp.any(list_piece == (target_piece // BLOCK)[:, None], axis=1)
    extra = has_target & jnp.logical_not(target_listed)
    block_used = jnp.any(list_piece[:, :, None] == tile_ids[None, None, :], axis=1)
    logits = (
        jnp.einsum("qe,pe->qp", query_piece, paired, preferred_element_type=jnp.float32)
        * scale_factor
    )
    chosen = jnp.repeat(block_used, BLOCK, axis=1)
    masked = jnp.where(chosen, logits, masked_floor)
    part_max = jnp.max(masked, axis=1)
    part_sum = jnp.sum(jnp.where(chosen, jnp.exp(logits - part_max[:, None]), 0.0), axis=1)
    extra_logit = jnp.where(extra, target_logit, masked_floor)
    full_max = jnp.maximum(part_max, extra_logit)
    full_sum = part_sum * jnp.exp(part_max - full_max) + jnp.where(
        extra, jnp.exp(target_logit - full_max), 0.0
    )
    kept_target = jnp.where(has_target, target_logit, 0.0)
    partial_stats = (full_max, full_sum, kept_target)
    own_first = lax.axis_index("dp") * query_count
    merged = joined(partial_stats, "dp", combine_stats)
    own_max = lax.dynamic_slice_in_dim(merged[0], own_first, query_count, 0)
    own_sum = lax.dynamic_slice_in_dim(merged[1], own_first, query_count, 0)
    own_target = lax.dynamic_slice_in_dim(merged[2], own_first, query_count, 0)
    query_loss = own_max + jnp.log(own_sum) - own_target
    return query_loss[None, :]


def solution(mesh):
    in_specs = (
        P("fsdp", ("dp", "query"), None),
        P("fsdp", ("dp", "query"), None),
        P("fsdp", None),
        P("fsdp", ("dp", "query")),
        P("fsdp", ("dp", "query"), None),
        P("fsdp", ("dp", "query")),
    )
    out_specs = P("fsdp", ("dp", "query"))
    return jax.shard_map(local, mesh=mesh, in_specs=in_specs, out_specs=out_specs, check_vma=False)
```

profile of v0, /device:TPU:0, one launch (start us, length us, event | category | flops | bytes accessed | tf_op | source)
XLA Modules:
  0.0 134.4 jit_solution(7281358317978102285)
XLA Ops:
  6.5 0.0 copy-start
  6.5 0.0 all-gather.11.cloned.1.call-start
  6.5 0.7 all-gather.11.cloned.1.call-update
  7.3 0.0 copy-start.4
  7.3 0.0 all-gather.15.cloned.1.call-start
  7.3 26.9 %all-gather.11.cloned.1.call-done = bf16[1024,1024]{1,0:T(8,128)(2,1)} async-done(((bf16[256,1024]{1,0:T(8,128)(2,1)}), bf16[1024,1024]{1,0:T(8,128)(2,1)}) %all-gather.11.cloned.1.call-update) | async-done | bytes 2097168 | tf_op jit(solution)/shard_map/all_gather | solution.py:35
  34.2 0.0 copy-done
  34.2 0.0 copy-start.3
  34.2 3.2 %convolution_convert_fusion = bf16[256,1024]{1,0:T(8,128)(2,1)} fusion(bf16[1024,1024]{1,0:T(8,128)(2,1)} %all-gather.11.cloned.1.call-done, bf16[1,256,1024]{2,1,0:T(8,128)(2,1)S(1)} %copy-done), kind=kOutput, calls=%fused_computation.9 | convolution fusion | flops 537133056 | bytes 3145728 | tf_op jit(solution)/shard_map/dot_general | solution.py:37
  37.5 0.0 copy-start.5
  37.5 0.0 copy-start.6
  37.5 0.0 all-gather.15.cloned.1.call-update
  37.5 0.0 all-gather.13.cloned.1.call-start
  37.6 0.0 copy-done.4
  37.6 0.0 copy-done.3
  37.6 1.2 convolution_convert_fusion.1
  38.8 0.0 all-gather.13.cloned.1.call-update
  39.5 0.0 copy-done.5
  39.5 10.8 %all-gather = s32[1,512]{1,0:T(1,128)S(1)} all-gather(s32[1,128]{1,0:T(1,128)S(1)} %copy-done.5), channel_id=2, replica_groups=mesh['dp'=4,'fsdp'=4,'query'=2] {'dp'}, dimensions={1}, use_global_device_ids=true | all-gather | bytes 2560 | tf_op jit(solution)/shard_map/all_gather | solution.py:52
  50.3 0.0 copy-done.6
  50.3 0.1 reshape.28
  50.4 7.6 %all_gather.33 = s32[512,2]{0,1:T(2,128)S(1)} all-gather(s32[128,2]{0,1:T(2,128)S(1)} %reshape.28), channel_id=1, replica_groups=mesh['dp'=4,'fsdp'=4,'query'=2] {'dp'}, dimensions={0}, use_global_device_ids=true | all-gather | bytes 5120 | tf_op jit(solution)/shard_map/all_gather | solution.py:51
  58.0 0.1 compare_reduce_fusion
  58.1 0.9 all-gather.15.cloned.1.call-done
  59.0 4.1 %gather_fusion = bf16[512,1024]{1,0:T(8,128)(2,1)S(1)} fusion(bf16[512,1024]{1,0:T(8,128)(2,1)} %all-gather.15.cloned.1.call-done, s32[1024]{0:T(1024)S(1)} %pad_clamp_fusion), kind=kCustom, calls=%fused_computation | custom fusion | bytes 2099200 | tf_op jit(solution)/shard_map/jit(_take)/gather | solution.py:55
  63.1 0.0 copy-start.1
  63.1 25.4 %all-gather.13.cloned.1.call-done = bf16[512,1024]{1,0:T(8,128)(2,1)} async-done(((bf16[128,1024]{1,0:T(8,128)(2,1)}), bf16[512,1024]{1,0:T(8,128)(2,1)}) %all-gather.13.cloned.1.call-update) | async-done | bytes 1048592 | tf_op jit(solution)/shard_map/all_gather | solution.py:50
  88.5 0.0 copy-start.2
  88.5 1.8 %multiply_reduce_fusion = f32[512]{0:T(512)S(1)} fusion(bf16[512,1024]{1,0:T(8,128)(2,1)} %all-gather.13.cloned.1.call-done, bf16[512,1024]{1,0:T(8,128)(2,1)S(1)} %gather_fusion, pred[512]{0:T(512)(128)(4,1)S(1)} %get-tuple-element.204), kind=kLoop, calls=%fused_computation.5 | loop fusion | flops 2620928 | bytes 2099712 | tf_op jit(solution)/shard_map/reduce_sum | solution.py:57
  90.4 0.0 copy-done.1
  90.4 0.0 copy-done.2
  90.4 0.8 fusion
  91.2 0.2 fusion.1
  91.4 11.9 %all-gather.4 = f32[4,1,512]{2,1,0:T(1,128)S(1)} all-gather(f32[1,1,512]{2,1,0:T(1,128)S(1)} %bitcast.62), channel_id=3, replica_groups=mesh['dp'=4,'fsdp'=4,'query'=2] {'dp'}, dimensions={0}, use_global_device_ids=true | all-gather | bytes 10240 | tf_op jit(solution)/shard_map/all_gather | solution.py:13
  103.3 11.9 %all-gather.5 = f32[4,1,512]{2,1,0:T(1,128)S(1)} all-gather(f32[1,1,512]{2,1,0:T(1,128)S(1)} %bitcast.61), channel_id=4, replica_groups=mesh['dp'=4,'fsdp'=4,'query'=2] {'dp'}, dimensions={0}, use_global_device_ids=true | all-gather | bytes 10240 | tf_op jit(solution)/shard_map/all_gather | solution.py:13
  115.2 11.9 %all-gather.6 = f32[4,1,512]{2,1,0:T(1,128)S(1)} all-gather(f32[1,1,512]{2,1,0:T(1,128)S(1)} %bitcast.60), channel_id=5, replica_groups=mesh['dp'=4,'fsdp'=4,'query'=2] {'dp'}, dimensions={0}, use_global_device_ids=true | all-gather | bytes 10240 | tf_op jit(solution)/shard_map/all_gather | solution.py:13
  127.1 0.3 while.19
  127.3 0.6 subtract_bitcast_fusion
  (26 shorter events, 0.2 us)
Async XLA Ops:
  6.5 27.7 %copy-start = (bf16[1,256,1024]{2,1,0:T(8,128)(2,1)S(1)}, bf16[1,256,1024]{2,1,0:T(8,128)(2,1)}, u32[]{:S(2)}) copy-start(bf16[1,256,1024]{2,1,0:T(8,128)(2,1)} %param.9) | copy-start | bytes 1572868
  6.5 27.7 %all-gather.11.cloned.1.call-start = ((), (), s32[]{:S(2)}) async-start(), calls=%async_computation | async-start | bytes 2621440 | tf_op jit(solution)/shard_map/all_gather | solution.py:35
  7.3 30.3 %copy-start.4 = (bf16[1,128,1024]{2,1,0:T(8,128)(2,1)S(1)}, bf16[1,128,1024]{2,1,0:T(8,128)(2,1)}, u32[]{:S(2)}) copy-start(bf16[1,128,1024]{2,1,0:T(8,128)(2,1)} %param.8) | copy-start | bytes 786436
  7.3 51.7 %all-gather.15.cloned.1.call-start = ((), (), s32[]{:S(2)}) async-start(), calls=%async_computation.2 | async-start | bytes 1572864 | tf_op jit(solution)/shard_map/all_gather | solution.py:40
  34.2 3.3 %copy-start.3 = (bf16[1024,1024]{1,0:T(8,128)(2,1)S(1)}, bf16[1024,1024]{1,0:T(8,128)(2,1)}, u32[]{:S(2)}) copy-start(bf16[1024,1024]{1,0:T(8,128)(2,1)} %all-gather.11.cloned.1.call-done) | copy-start | bytes 6291460
  37.5 2.0 %copy-start.5 = (s32[1,128]{1,0:T(1,128)S(1)}, s32[1,128]{1,0:T(1,128)}, u32[]{:S(2)}) copy-start(s32[1,128]{1,0:T(1,128)} %param.11) | copy-start | bytes 1540
  37.5 12.8 %copy-start.6 = (s32[1,1,2]{2,1,0:T(1,128)S(1)}, s32[1,1,2]{2,1,0:T(1,128)}, u32[]{:S(2)}) copy-start(s32[1,1,2]{2,1,0:T(1,128)} %param.12) | copy-start | bytes 28
  37.5 51.0 %all-gather.13.cloned.1.call-start = ((), (), s32[]{:S(2)}) async-start(), calls=%async_computation.1 | async-start | bytes 1310720 | tf_op jit(solution)/shard_map/all_gather | solution.py:50
  63.1 27.3 %copy-start.1 = (bf16[512,1024]{1,0:T(8,128)(2,1)S(1)}, bf16[512,1024]{1,0:T(8,128)(2,1)}, u32[]{:S(2)}) copy-start(bf16[512,1024]{1,0:T(8,128)(2,1)} %all-gather.15.cloned.1.call-done) | copy-start | bytes 3145732
  88.5 1.9 %copy-start.2 = (bf16[512,1024]{1,0:T(8,128)(2,1)S(1)}, bf16[512,1024]{1,0:T(8,128)(2,1)}, u32[]{:S(2)}) copy-start(bf16[512,1024]{1,0:T(8,128)(2,1)} %all-gather.13.cloned.1.call-done) | copy-start | bytes 3145732
Sparse Core Ops, SparseCore 0:
  8.9 25.2 all-gather.10
  37.6 21.2 all-gather.14
  60.6 27.9 all-gather.12
where the time goes:
time: 135 us; the launch traced here: 134 us
  waiting for transfers between devices  54 us (40%)
  blocking collectives  54 us (40%)
  between operations  13.9 us (10%)
  matrix products  5.21 us (4%)
  local copies, waits for them, and re-layouts  4.26 us (3%)
  other arithmetic  2.9 us (2%)
    all_gather x3, blocking collectives, joined(): gathered = jax.tree.map(lambda a: lax.all_gather(a, axis), part)  35.6 us
    all_gather x1, waiting for transfers between devices, local(): shard_rows = lax.all_gather(head_weight, 'fsdp', axis=0, tiled=True)  26.9 us
    all_gather x1, waiting for transfers between devices, local(): query_piece = lax.all_gather(query_proj, 'dp', axis=0, tiled=True)  25.4 us
    all_gather x1, blocking collectives, local(): target_piece = lax.all_gather(targets, 'dp', axis=0, tiled=True)  10.8 us
    all_gather x1, blocking collectives, local(): list_piece = lax.all_gather(row_lists, 'dp', axis=0, tiled=True)  7.56 us
    gather x1, local copies, waits for them, and re-layouts, local(): jnp.take(paired, jnp.clip(local_target, 0, pair_count - 1), axis=0)  4.09 us
    dot_general x1, matrix products, local(): jnp.dot(passage_rows, shard_rows, preferred_element_type=jnp.float32)  3.25 us
  transfers between devices with their start and end apart: 3, of which 3 were waited for; matrix products, arithmetic and copies ran while one was open for 4% of the time, Pallas kernels for 0%

commit v1 on v0

v1 whole, which is shorter than its diff:
```python
import functools

import jax
import jax.numpy as jnp
from jax import lax
from jax.experimental import pallas as pl
from jax.experimental.pallas import tpu as pltpu
from jax.sharding import PartitionSpec as P

BLOCK = 128
CORES = 2
PIECES = 2
MASKED = -1e30
MESH = pl.DeviceIdType.MESH


def kernel(
    sizes, q_ref, p_ref, w_ref, pos_ref, ids_ref, count_ref, out_ref,
    q_all, p_all, p_proj, w_all, meta, stats_out, stats_in,
    local_sem, q_send, q_recv, p_send, p_recv, own_send, own_recv,
    wy_send, wy_recv, wc_send, wc_recv, meta_send, meta_recv, st_send, st_recv,
):
    n, shards, pairs, max_list = sizes
    towers = shards // CORES
    rows_w = w_ref.shape[0]
    rows_p = p_ref.shape[1]
    width = q_ref.shape[2]
    piece_q = BLOCK // PIECES
    piece_w = rows_w // PIECES
    scale = width ** -0.5
    z = lax.axis_index("dp")
    f = lax.axis_index("fsdp")
    x = lax.axis_index("query")
    core = lax.rem(f, CORES)
    mate = f + 1 - 2 * core

    def remote(src, dst, send, recv, where):
        return pltpu.make_async_remote_copy(
            src_ref=src, dst_ref=dst, send_sem=send, recv_sem=recv,
            device_id=where, device_id_type=MESH,
        )

    def shard_rows(shard, c):
        start = pl.multiple_of(shard * rows_w + c * piece_w, piece_w)
        return w_all.at[pl.ds(start, piece_w)]

    own_w = w_all.at[pl.ds(pl.multiple_of(f * rows_w, rows_w), rows_w)]
    own_p = p_all.at[pl.ds(pl.multiple_of(x * rows_p, rows_p), rows_p)]
    locals_ = [
        pltpu.make_async_copy(w_ref, own_w, local_sem.at[0]),
        pltpu.make_async_copy(p_ref.at[0], own_p, local_sem.at[1]),
        pltpu.make_async_copy(q_ref.at[0], q_all.at[z], local_sem.at[2]),
    ]
    for copy in locals_:
        copy.start()

    barrier = pltpu.get_barrier_semaphore()
    friends = [{"dp": lax.rem(z + o, n)} for o in range(1, n)]
    friends += [{"query": lax.rem(x + o, pairs)} for o in range(1, pairs)]
    friends += [{"fsdp": lax.rem(f + CORES * o, shards)} for o in range(1, towers)]
    friends += [{"fsdp": mate}]
    for friend in friends:
        pl.semaphore_signal(barrier, inc=1, device_id=friend, device_id_type=MESH)

    meta[z, 0:1, :] = pos_ref[...]
    live = count_ref[0, 0]
    for l in range(max_list):
        entry = jnp.where(l < live, ids_ref[0, 0, l], -1)
        meta[z, l + 1:l + 2, :] = jnp.full((1, BLOCK), entry, jnp.int32)
    pl.semaphore_wait(barrier, len(friends))

    def q_copy(way, step, h):
        block = z - step if way == 0 else z + step
        block = jnp.clip(block, 0, n - 1)
        view = q_all.at[block, pl.ds(h * piece_q, piece_q)]
        src = q_ref.at[0, pl.ds(h * piece_q, piece_q)] if step == 0 else view
        target = jnp.minimum(z + 1, n - 1) if way == 0 else jnp.maximum(z - 1, 0)
        return remote(src, view, q_send.at[way, step, h], q_recv.at[way, step, h], {"dp": target})

    def q_sends(way, step):
        if way == 0:
            return (z + 1 < n) & (z >= step)
        return (z >= 1) & (z + step < n)

    def q_wait(way, step, h):
        block = z - 1 - step if way == 0 else z + 1 + step
        block = jnp.clip(block, 0, n - 1)
        view = q_all.at[block, pl.ds(h * piece_q, piece_q)]
        pltpu.make_async_copy(view, view, q_recv.at[way, step, h]).wait()

    def q_receives(way, step):
        return z - 1 - step >= 0 if way == 0 else z + 1 + step < n

    for h in range(PIECES):
        for way in range(2):
            @pl.when(q_sends(way, 0))
            def _():
                q_copy(way, 0, h).start()

    sent = []
    for c in range(PIECES):
        for o in range(1, towers):
            copy = remote(
                w_ref.at[pl.ds(c * piece_w, piece_w)], shard_rows(f, c),
                wy_send.at[o - 1, c], wy_recv.at[o - 1, c],
                {"fsdp": lax.rem(f + CORES * o, shards)},
            )
            copy.start()
            sent.append(copy)
    for o in range(1, pairs):
        copy = remote(
            p_ref.at[0], own_p, p_send.at[o - 1], p_recv.at[o - 1],
            {"query": lax.rem(x + o, pairs)},
        )
        copy.start()
        sent.append(copy)
    own_copy = remote(w_ref, own_w, own_send, own_recv, {"fsdp": mate})
    own_copy.start()
    sent.append(own_copy)
    for o in range(1, n):
        copy = remote(
            meta.at[z], meta.at[z], meta_send.at[o - 1], meta_recv.at[o - 1],
            {"dp": lax.rem(z + o, n)},
        )
        copy.start()
        sent.append(copy)

    def pass_queries(step, h):
        for way in range(2):
            @pl.when(q_receives(way, step))
            def _():
                q_wait(way, step, h)

            @pl.when(q_sends(way, step + 1))
            def _():
                q_copy(way, step + 1, h).start()

    def pass_weights(c):
        for o in range(1, towers):
            shard = lax.rem(f + shards - CORES * o, shards)
            view = shard_rows(shard, c)
            pltpu.make_async_copy(view, view, wy_recv.at[o - 1, c]).wait()
            copy = remote(view, view, wc_send.at[o - 1, c], wc_recv.at[o - 1, c], {"fsdp": mate})
            copy.start()
            sent.append(copy)

    events = [(step * PIECES + h, 0, (step, h)) for step in range(n - 2) for h in range(PIECES)]
    events += [(2 * c + 1, 1, c) for c in range(PIECES)]
    for _, kind, what in sorted(events):
        if kind == 0:
            pass_queries(*what)
        else:
            pass_weights(what)

    for copy in locals_:
        copy.wait()
    other_w = w_all.at[pl.ds(pl.multiple_of(mate * rows_w, rows_w), rows_w)]
    pltpu.make_async_copy(other_w, other_w, own_recv).wait()
    for c in range(PIECES):
        for o in range(1, towers):
            view = shard_rows(lax.rem(mate + shards - CORES * o, shards), c)
            pltpu.make_async_copy(view, view, wc_recv.at[o - 1, c]).wait()

    def project(rows):
        return jnp.dot(rows, w_all[...], preferred_element_type=jnp.float32).astype(jnp.bfloat16)

    for o in range(pairs):
        holder = lax.rem(x + pairs - o, pairs)
        part = pl.ds(pl.multiple_of(holder * rows_p, rows_p), rows_p)
        if o:
            view = p_all.at[part]
            pltpu.make_async_copy(view, view, p_recv.at[o - 1]).wait()
        p_proj[part, :] = project(p_all[part, :])

    for o in range(1, n):
        view = meta.at[lax.rem(z + n - o, n)]
        pltpu.make_async_copy(view, view, meta_recv.at[o - 1]).wait()

    tiles = pairs * rows_p // BLOCK
    first_tile = z * tiles
    row_index = lax.broadcasted_iota(jnp.int32, (BLOCK, BLOCK), 0)

    def stats_copy(block):
        return remote(
            stats_out.at[block], stats_in.at[z], st_send.at[block], st_recv.at[z], {"dp": block}
        )

    def meet(t, carry):
        away = lax.div(t + 1, 2)
        way = lax.rem(t + 1, 2)
        place = jnp.where(way == 0, z - away, z + away)
        block = jnp.clip(place, 0, n - 1)

        @pl.when((place >= 0) & (place < n))
        def _():
            @pl.when(away == n - 1)
            def _():
                for h in range(PIECES):
                    view = q_all.at[block, pl.ds(h * piece_q, piece_q)]
                    pltpu.make_async_copy(view, view, q_recv.at[way, n - 2, h]).wait()

            q_proj = project(q_all[block])
            logits = lax.dot_general(
                p_proj[...], q_proj, (((1,), (1,)), ((), ())),
                preferred_element_type=jnp.float32,
            ) * scale
            info = meta[block]
            target = info[0:1, :]
            top = jnp.full((1, BLOCK), MASKED, jnp.float32)
            target_logit = jnp.zeros((1, BLOCK), jnp.float32)
            picks = []
            for k in range(tiles):
                tile = logits[k * BLOCK:(k + 1) * BLOCK, :]
                listed = info[1:2, :] == first_tile + k
                for l in range(1, max_list):
                    listed = listed | (info[l + 1:l + 2, :] == first_tile + k)
                is_target = row_index == target - (first_tile + k) * BLOCK
                chosen = listed | is_target
                picks.append((tile, chosen))
                top = jnp.maximum(
                    top, jnp.max(jnp.where(chosen, tile, MASKED), axis=0, keepdims=True)
                )
                target_logit += jnp.sum(jnp.where(is_target, tile, 0.0), axis=0, keepdims=True)
            total = jnp.zeros((1, BLOCK), jnp.float32)
            for tile, chosen in picks:
                total += jnp.sum(
                    jnp.where(chosen, jnp.exp(tile - top), 0.0), axis=0, keepdims=True
                )

            @pl.when(t == 0)
            def _():
                stats_in[z, 0:1, :] = top
                stats_in[z, 1:2, :] = total
                stats_in[z, 2:3, :] = target_logit

            @pl.when(t > 0)
            def _():
                stats_out[block, 0:1, :] = top
                stats_out[block, 1:2, :] = total
                stats_out[block, 2:3, :] = target_logit
                stats_copy(block).start()

        return carry

    lax.fori_loop(0, 2 * n - 1, meet, 0)

    for o in range(1, n):
        view = stats_in.at[lax.rem(z + o, n)]
        pltpu.make_async_copy(view, view, st_recv.at[lax.rem(z + o, n)]).wait()
    top = stats_in[0, 0:1, :]
    for i in range(1, n):
        top = jnp.maximum(top, stats_in[i, 0:1, :])
    total = jnp.zeros((1, BLOCK), jnp.float32)
    target_logit = jnp.zeros((1, BLOCK), jnp.float32)
    for i in range(n):
        total += stats_in[i, 1:2, :] * jnp.exp(stats_in[i, 0:1, :] - top)
        target_logit += stats_in[i, 2:3, :]
    out_ref[...] = top + jnp.log(total) - target_logit

    for copy in sent:
        copy.wait_send()
    for step in range(n - 1):
        for way in range(2):
            @pl.when(q_sends(way, step))
            def _():
                for h in range(PIECES):
                    q_copy(way, step, h).wait_send()
    for o in range(1, n):
        stats_copy(lax.rem(z + o, n)).wait_send()


def local(sizes, queries, passages, head_weight, positives, negative_ids, negative_count):
    n, shards, pairs, max_list = sizes
    towers = shards // CORES
    width = queries.shape[2]
    rows_p = passages.shape[1]
    meta_rows = -(-(max_list + 1) // 8) * 8
    hops = max(n - 1, 1)
    dma = pltpu.SemaphoreType.DMA
    far = max(towers - 1, 1)
    return pl.pallas_call(
        functools.partial(kernel, sizes),
        out_shape=jax.ShapeDtypeStruct((1, BLOCK), jnp.float32),
        in_specs=[
            pl.BlockSpec(memory_space=pl.ANY),
            pl.BlockSpec(memory_space=pl.ANY),
            pl.BlockSpec(memory_space=pl.ANY),
            pl.BlockSpec(memory_space=pltpu.VMEM),
            pl.BlockSpec(memory_space=pltpu.SMEM),
            pl.BlockSpec(memory_space=pltpu.SMEM),
        ],
        out_specs=pl.BlockSpec(memory_space=pltpu.VMEM),
        scratch_shapes=[
            pltpu.VMEM((n, BLOCK, width), jnp.bfloat16),
            pltpu.VMEM((pairs * rows_p, width), jnp.bfloat16),
            pltpu.VMEM((pairs * rows_p, width), jnp.bfloat16),
            pltpu.VMEM((shards * head_weight.shape[0], width), jnp.bfloat16),
            pltpu.VMEM((n, meta_rows, BLOCK), jnp.int32),
            pltpu.VMEM((n, 8, BLOCK), jnp.float32),
            pltpu.VMEM((n, 8, BLOCK), jnp.float32),
            dma((3,)),
            dma((2, hops, PIECES)), dma((2, hops, PIECES)),
            dma((max(pairs - 1, 1),)), dma((max(pairs - 1, 1),)),
            dma, dma,
            dma((far, PIECES)), dma((far, PIECES)),
            dma((far, PIECES)), dma((far, PIECES)),
            dma((hops,)), dma((hops,)),
            dma((n,)), dma((n,)),
        ],
        compiler_params=pltpu.CompilerParams(
            collective_id=0, has_side_effects=True, vmem_limit_bytes=40 * 1024 * 1024
        ),
        name="retriever_loss",
    )(queries, passages, head_weight, positives, negative_ids, negative_count)


def solution(mesh):
    in_specs = (
        P("fsdp", ("dp", "query"), None),
        P("fsdp", ("dp", "query"), None),
        P("fsdp", None),
        P("fsdp", ("dp", "query")),
        P("fsdp", ("dp", "query"), None),
        P("fsdp", ("dp", "query")),
    )
    out_specs = P("fsdp", ("dp", "query"))

    def whole(queries, passages, head_weight, positives, negative_ids, negative_count):
        sizes = (
            mesh.shape["dp"], mesh.shape["fsdp"], mesh.shape["query"], negative_ids.shape[2]
        )
        return jax.shard_map(
            functools.partial(local, sizes),
            mesh=mesh, in_specs=in_specs, out_specs=out_specs, check_vma=False,
        )(queries, passages, head_weight, positives, negative_ids, negative_count)

    return whole
```

time: 135 us -> 33 us (0.24)
  blocking collectives: 54 us -> 0 us
  waiting for transfers between devices: 54 us -> 0 us
  Pallas kernels: 0 us -> 28.3 us
  between operations: 13.9 us -> 0.72 us
  matrix products: 5.21 us -> 0 us
  other arithmetic: 2.9 us -> 0 us
    all_gather x5 -> x0, blocking collectives: 54 us -> none  [the longest x3 35.6 us: joined(): gathered = jax.tree.map(lambda a: lax.all_gather(a, axis), part)]
    all_gather x3 -> x0, waiting for transfers between devices: 53.3 us -> none  [the longest x1 26.9 us: local(): shard_rows = lax.all_gather(head_weight, 'fsdp', axis=0, tiled=True)]
    pallas_call x0 -> x1, Pallas kernels: none -> 28.3 us  [local(): pl.pallas_call(functools.partial(kernel, sizes), out_shape=jax.ShapeDtype...]
    dot_general x3 -> x0, matrix products: 5.21 us -> none  [the longest x1 3.25 us: local(): jnp.dot(passage_rows, shard_rows, preferred_element_type=jnp.float32)]
    gather x1 -> x0, local copies, waits for them, and re-layouts: 4.09 us -> none  [local(): jnp.take(paired, jnp.clip(local_target, 0, pair_count - 1), axis=0)]
    unnamed x17 -> x11, local copies, waits for them, and re-layouts: 0.04 us -> 3.55 us
    reduce_sum x2 -> x0, other arithmetic: 2.05 us -> none  [the longest x1 1.83 us: local(): jnp.sum(query_piece.astype(jnp.float32) * target_rows.astype(jnp.float32)...]
  transfers between devices with their start and end apart: 3 -> 0, of which waited for: 3 -> 0; matrix products, arithmetic and copies ran while one was open for 4% -> 0% of each run, Pallas kernels for 0% -> 0%
where the time goes in v1:
time: 33 us; the launch traced here: 32.6 us
  Pallas kernels  28.3 us (86%)
  local copies, waits for them, and re-layouts  3.55 us (11%)
  between operations  0.72 us (2%)
    pallas_call x1, Pallas kernels, local(): pl.pallas_call(functools.partial(kernel, sizes), out_shape=jax.ShapeDtype...  28.3 us
    unnamed x11, local copies, waits for them, and re-layouts  3.55 us

profile of v1, /device:TPU:0, one launch (start us, length us, event | category | flops | bytes accessed | tf_op | source)
XLA Modules:
  0.0 32.6 jit_solution(7659847711779482105)
XLA Ops:
  0.0 0.0 copy-start.4
  0.0 0.0 copy-start.3
  0.7 0.0 copy-done.4
  0.7 0.0 copy-done.3
  0.7 0.0 copy-start
  0.7 1.0 %copy-done = bf16[1,256,1024]{2,1,0:T(8,128)(2,1)S(1)} copy-done((bf16[1,256,1024]{2,1,0:T(8,128)(2,1)S(1)}, bf16[1,256,1024]{2,1,0:T(8,128)(2,1)}, u32[]{:S(2)}) %copy-start) | copy-done | bytes 524312
  1.7 0.0 copy-start.1
  1.7 1.0 %copy-done.1 = bf16[256,1024]{1,0:T(8,128)(2,1)S(1)} copy-done((bf16[256,1024]{1,0:T(8,128)(2,1)S(1)}, bf16[256,1024]{1,0:T(8,128)(2,1)}, u32[]{:S(2)}) %copy-start.1) | copy-done | bytes 524312
  2.8 0.0 copy-start.2
  2.8 0.9 %copy-done.2 = bf16[1,128,1024]{2,1,0:T(8,128)(2,1)S(1)} copy-done((bf16[1,128,1024]{2,1,0:T(8,128)(2,1)S(1)}, bf16[1,128,1024]{2,1,0:T(8,128)(2,1)}, u32[]{:S(2)}) %copy-start.2) | copy-done | bytes 262168
  3.7 28.3 %retriever_loss.1 = f32[1,128]{1,0:T(1,128)S(1)} custom-call(bf16[1,128,1024]{2,1,0:T(8,128)(2,1)S(1)} %copy-done.2, bf16[1,256,1024]{2,1,0:T(8,128)(2,1)S(1)} %copy-done, bf16[256,1024]{1,0:T(8,128)(2,1)S(1)} %copy-done.1, s32[1,128]{1,0:T(1,128)S(1)} %copy-done.3, s32[1,1,2]{2,1,0:T(1,128)S(1)} %copy-done.4, s32[1,1]{1,0:T(1,128)S(6)} %copy.8.count_ref), custom_call_target="tpu_custom_call" | custom-call | tf_op jit(solution)/shard_map/retriever_loss/pallas_call | solution.py:281
  32.1 0.5 %copy.9 = f32[1,128]{1,0:T(1,128)} copy(f32[1,128]{1,0:T(1,128)S(1)} %retriever_loss.1) | data formatting | bytes 1024
Async XLA Ops:
  0.0 0.7 %copy-start.4 = (s32[1,1,2]{2,1,0:T(1,128)S(1)}, s32[1,1,2]{2,1,0:T(1,128)}, u32[]{:S(2)}) copy-start(s32[1,1,2]{2,1,0:T(1,128)} %ids_ref.1) | copy-start | bytes 28
  0.0 0.7 %copy-start.3 = (s32[1,128]{1,0:T(1,128)S(1)}, s32[1,128]{1,0:T(1,128)}, u32[]{:S(2)}) copy-start(s32[1,128]{1,0:T(1,128)} %pos_ref.1) | copy-start | bytes 1540
  0.7 1.0 %copy-start = (bf16[1,256,1024]{2,1,0:T(8,128)(2,1)S(1)}, bf16[1,256,1024]{2,1,0:T(8,128)(2,1)}, u32[]{:S(2)}) copy-start(bf16[1,256,1024]{2,1,0:T(8,128)(2,1)} %p_ref.1) | copy-start | bytes 1572868
  1.7 1.0 %copy-start.1 = (bf16[256,1024]{1,0:T(8,128)(2,1)S(1)}, bf16[256,1024]{1,0:T(8,128)(2,1)}, u32[]{:S(2)}) copy-start(bf16[256,1024]{1,0:T(8,128)(2,1)} %w_ref.1) | copy-start | bytes 1572868
  2.8 0.9 %copy-start.2 = (bf16[1,128,1024]{2,1,0:T(8,128)(2,1)S(1)}, bf16[1,128,1024]{2,1,0:T(8,128)(2,1)}, u32[]{:S(2)}) copy-start(bf16[1,128,1024]{2,1,0:T(8,128)(2,1)} %q_ref.1) | copy-start | bytes 786436

commit v2 on v1

--- a/solution.py
+++ b/solution.py
@@ -16,7 +16,7 @@
 
 def kernel(
     sizes, q_ref, p_ref, w_ref, pos_ref, ids_ref, count_ref, out_ref,
-    q_all, p_all, p_proj, w_all, meta, stats_out, stats_in,
+    q_all, p_all, p_proj, w_all, meta, stats_out, stats_in, ids_own, count_own,
     local_sem, q_send, q_recv, p_send, p_recv, own_send, own_recv,
     wy_send, wy_recv, wc_send, wc_recv, meta_send, meta_recv, st_send, st_recv,
 ):
@@ -46,6 +46,13 @@
 
     own_w = w_all.at[pl.ds(pl.multiple_of(f * rows_w, rows_w), rows_w)]
     own_p = p_all.at[pl.ds(pl.multiple_of(x * rows_p, rows_p), rows_p)]
+    lists_ = [
+        pltpu.make_async_copy(pos_ref, meta.at[z, pl.ds(0, 1)], local_sem.at[3]),
+        pltpu.make_async_copy(ids_ref, ids_own, local_sem.at[4]),
+        pltpu.make_async_copy(count_ref, count_own, local_sem.at[5]),
+    ]
+    for copy in lists_:
+        copy.start()
     locals_ = [
         pltpu.make_async_copy(w_ref, own_w, local_sem.at[0]),
         pltpu.make_async_copy(p_ref.at[0], own_p, local_sem.at[1]),
@@ -62,10 +69,11 @@
     for friend in friends:
         pl.semaphore_signal(barrier, inc=1, device_id=friend, device_id_type=MESH)
 
-    meta[z, 0:1, :] = pos_ref[...]
-    live = count_ref[0, 0]
+    for copy in lists_:
+        copy.wait()
+    live = count_own[0, 0]
     for l in range(max_list):
-        entry = jnp.where(l < live, ids_ref[0, 0, l], -1)
+        entry = jnp.where(l < live, ids_own[0, 0, l], -1)
         meta[z, l + 1:l + 2, :] = jnp.full((1, BLOCK), entry, jnp.int32)
     pl.semaphore_wait(barrier, len(friends))
 
@@ -282,13 +290,8 @@
         functools.partial(kernel, sizes),
         out_shape=jax.ShapeDtypeStruct((1, BLOCK), jnp.float32),
         in_specs=[
-            pl.BlockSpec(memory_space=pl.ANY),
-            pl.BlockSpec(memory_space=pl.ANY),
-            pl.BlockSpec(memory_space=pl.ANY),
-            pl.BlockSpec(memory_space=pltpu.VMEM),
-            pl.BlockSpec(memory_space=pltpu.SMEM),
-            pl.BlockSpec(memory_space=pltpu.SMEM),
-        ],
+            pl.BlockSpec(memory_space=pltpu.HBM),
+        ] * 6,
         out_specs=pl.BlockSpec(memory_space=pltpu.VMEM),
         scratch_shapes=[
             pltpu.VMEM((n, BLOCK, width), jnp.bfloat16),
@@ -298,7 +301,9 @@
             pltpu.VMEM((n, meta_rows, BLOCK), jnp.int32),
             pltpu.VMEM((n, 8, BLOCK), jnp.float32),
             pltpu.VMEM((n, 8, BLOCK), jnp.float32),
-            dma((3,)),
+            pltpu.SMEM(negative_ids.shape, jnp.int32),
+            pltpu.SMEM(negative_count.shape, jnp.int32),
+            dma((6,)),
             dma((2, hops, PIECES)), dma((2, hops, PIECES)),
             dma((max(pairs - 1, 1),)), dma((max(pairs - 1, 1),)),
             dma, dma,
@@ -308,7 +313,7 @@
             dma((n,)), dma((n,)),
         ],
         compiler_params=pltpu.CompilerParams(
-            collective_id=0, has_side_effects=True, vmem_limit_bytes=40 * 1024 * 1024
+            collective_id=0, has_side_effects=True, vmem_limit_bytes=64 * 1024 * 1024
         ),
         name="retriever_loss",
     )(queries, passages, head_weight, positives, negative_ids, negative_count)

time: 33 us -> 30.8 us (0.933)
  local copies, waits for them, and re-layouts: 3.55 us -> 1.19 us
    unnamed x11 -> x1, local copies, waits for them, and re-layouts: 3.55 us -> 1.19 us
where the time goes in v2:
time: 30.8 us; the launch traced here: 30.4 us
  Pallas kernels  28.5 us (93%)
  local copies, waits for them, and re-layouts  1.19 us (4%)
  between operations  0.66 us (2%)
    pallas_call x1, Pallas kernels, local(): pl.pallas_call(functools.partial(kernel, sizes), out_shape=jax.ShapeDtype...  28.5 us
    unnamed x1, local copies, waits for them, and re-layouts  1.19 us

profile of v2, /device:TPU:0, one launch (start us, length us, event | category | flops | bytes accessed | tf_op | source)
XLA Modules:
  0.0 30.4 jit_solution(9344188270484733260)
XLA Ops:
  0.7 28.5 %retriever_loss.1 = f32[1,128]{1,0:T(1,128)} custom-call(bf16[1,128,1024]{2,1,0:T(8,128)(2,1)} %q_ref.1, bf16[1,256,1024]{2,1,0:T(8,128)(2,1)} %p_ref.1, bf16[256,1024]{1,0:T(8,128)(2,1)} %w_ref.1, s32[1,128]{1,0:T(1,128)} %pos_ref.1, s32[1,1,2]{2,1,0:T(1,128)} %ids_ref.1, s32[1,1]{1,0:T(1,128)S(6)} %copy.8.count_ref), custom_call_target="tpu_custom_call" | custom-call | tf_op jit(solution)/shard_map/retriever_loss/pallas_call | solution.py:289
  29.2 1.2 %copy.9 = f32[1,128]{1,0:T(1,128)} copy(f32[1,128]{1,0:T(1,128)} %retriever_loss.1) | data formatting | bytes 1024

commit v3 on v2

--- a/solution.py
+++ b/solution.py
@@ -17,8 +17,10 @@
 def kernel(
     sizes, q_ref, p_ref, w_ref, pos_ref, ids_ref, count_ref, out_ref,
     q_all, p_all, p_proj, w_all, meta, stats_out, stats_in, ids_own, count_own,
+    p_far, q_far, far_out,
     local_sem, q_send, q_recv, p_send, p_recv, own_send, own_recv,
     wy_send, wy_recv, wc_send, wc_recv, meta_send, meta_recv, st_send, st_recv,
+    pf_send, pf_recv, qf_send, qf_recv, mf_send, mf_recv, ex_send, ex_recv,
 ):
     n, shards, pairs, max_list = sizes
     towers = shards // CORES
@@ -33,6 +35,14 @@
     x = lax.axis_index("query")
     core = lax.rem(f, CORES)
     mate = f + 1 - 2 * core
+
+    short = n == 4 and pairs == 2
+    folded = (core == 1) if short else False
+    outer = (z == 0) | (z == n - 1)
+    far = lax.rem(z + 2, n)
+    beside = z + 1 - 2 * lax.rem(z, 2)
+    across = lax.rem(x + 1, pairs)
+    slots = n + 2 if short else n
 
     def remote(src, dst, send, recv, where):
         return pltpu.make_async_remote_copy(
@@ -66,6 +76,11 @@
     friends += [{"query": lax.rem(x + o, pairs)} for o in range(1, pairs)]
     friends += [{"fsdp": lax.rem(f + CORES * o, shards)} for o in range(1, towers)]
     friends += [{"fsdp": mate}]
+    if short:
+        friends += [{"dp": far, "query": across}]
+    for i in range(slots):
+        stats_in[i, 0:1, :] = jnp.full((1, BLOCK), MASKED, jnp.float32)
+        stats_in[i, 1:3, :] = jnp.zeros((2, BLOCK), jnp.float32)
     for friend in friends:
         pl.semaphore_signal(barrier, inc=1, device_id=friend, device_id_type=MESH)
 
@@ -86,9 +101,8 @@
         return remote(src, view, q_send.at[way, step, h], q_recv.at[way, step, h], {"dp": target})
 
     def q_sends(way, step):
-        if way == 0:
-            return (z + 1 < n) & (z >= step)
-        return (z >= 1) & (z + step < n)
+        there = (z + 1 < n) & (z >= step) if way == 0 else (z >= 1) & (z + step < n)
+        return there & jnp.logical_not(folded) if short and step == n - 2 else there
 
     def q_wait(way, step, h):
         block = z - 1 - step if way == 0 else z + 1 + step
@@ -98,6 +112,22 @@
 
     def q_receives(way, step):
         return z - 1 - step >= 0 if way == 0 else z + 1 + step < n
+
+    def qf_copy(h):
+        part = pl.ds(h * piece_q, piece_q)
+        return remote(
+            q_all.at[far, part], q_far.at[part], qf_send.at[h], qf_recv.at[h], {"query": across}
+        )
+
+    def pf_copy():
+        return remote(p_ref.at[0], p_far, pf_send, pf_recv, {"dp": beside})
+
+    def mf_copy():
+        return remote(meta.at[z], meta.at[n], mf_send, mf_recv, {"dp": far, "query": across})
+
+    def ex_copy(i):
+        where = {"dp": far, "query": across} if i else {"dp": far}
+        return remote(far_out.at[i], stats_in.at[n + i], ex_send.at[i], ex_recv.at[i], where)
 
     for h in range(PIECES):
         for way in range(2):
@@ -122,6 +152,11 @@
         )
         copy.start()
         sent.append(copy)
+    if short:
+        @pl.when(folded & outer)
+        def _():
+            pf_copy().start()
+            mf_copy().start()
     own_copy = remote(w_ref, own_w, own_send, own_recv, {"fsdp": mate})
     own_copy.start()
     sent.append(own_copy)
@@ -142,6 +177,11 @@
             @pl.when(q_sends(way, step + 1))
             def _():
                 q_copy(way, step + 1, h).start()
+
+        if short and step == 1:
+            @pl.when(folded & jnp.logical_not(outer))
+            def _():
+                qf_copy(h).start()
 
     def pass_weights(c):
         for o in range(1, towers):
@@ -193,13 +233,42 @@
             stats_out.at[block], stats_in.at[z], st_send.at[block], st_recv.at[z], {"dp": block}
         )
 
+    def block_stats(q_proj, held, info, tile_id):
+        logits = lax.dot_general(
+            held, q_proj, (((1,), (1,)), ((), ())), preferred_element_type=jnp.float32
+        ) * scale
+        target = info[0:1, :]
+        top = jnp.full((1, BLOCK), MASKED, jnp.float32)
+        target_logit = jnp.zeros((1, BLOCK), jnp.float32)
+        picks = []
+        for k in range(held.shape[0] // BLOCK):
+            tile = logits[k * BLOCK:(k + 1) * BLOCK, :]
+            listed = info[1:2, :] == tile_id + k
+            for l in range(1, max_list):
+                listed = listed | (info[l + 1:l + 2, :] == tile_id + k)
+            is_target = row_index == target - (tile_id + k) * BLOCK
+            chosen = listed | is_target
+            picks.append((tile, chosen))
+            top = jnp.maximum(
+                top, jnp.max(jnp.where(chosen, tile, MASKED), axis=0, keepdims=True)
+            )
+            target_logit += jnp.sum(jnp.where(is_target, tile, 0.0), axis=0, keepdims=True)
+        total = jnp.zeros((1, BLOCK), jnp.float32)
+        for tile, chosen in picks:
+            total += jnp.sum(jnp.where(chosen, jnp.exp(tile - top), 0.0), axis=0, keepdims=True)
+        return top, total, target_logit
+
     def meet(t, carry):
         away = lax.div(t + 1, 2)
         way = lax.rem(t + 1, 2)
         place = jnp.where(way == 0, z - away, z + away)
         block = jnp.clip(place, 0, n - 1)
 
-        @pl.when((place >= 0) & (place < n))
+        meets = (place >= 0) & (place < n)
+        if short:
+            meets = meets & jnp.logical_not(folded & (away == n - 1))
+
+        @pl.when(meets)
         def _():
             @pl.when(away == n - 1)
             def _():
@@ -207,33 +276,9 @@
                     view = q_all.at[block, pl.ds(h * piece_q, piece_q)]
                     pltpu.make_async_copy(view, view, q_recv.at[way, n - 2, h]).wait()
 
-            q_proj = project(q_all[block])
-            logits = lax.dot_general(
-                p_proj[...], q_proj, (((1,), (1,)), ((), ())),
-                preferred_element_type=jnp.float32,
-            ) * scale
-            info = meta[block]
-            target = info[0:1, :]
-            top = jnp.full((1, BLOCK), MASKED, jnp.float32)
-            target_logit = jnp.zeros((1, BLOCK), jnp.float32)
-            picks = []
-            for k in range(tiles):
-                tile = logits[k * BLOCK:(k + 1) * BLOCK, :]
-                listed = info[1:2, :] == first_tile + k
-                for l in range(1, max_list):
-                    listed = listed | (info[l + 1:l + 2, :] == first_tile + k)
-                is_target = row_index == target - (first_tile + k) * BLOCK
-                chosen = listed | is_target
-                picks.append((tile, chosen))
-                top = jnp.maximum(
-                    top, jnp.max(jnp.where(chosen, tile, MASKED), axis=0, keepdims=True)
-                )
-                target_logit += jnp.sum(jnp.where(is_target, tile, 0.0), axis=0, keepdims=True)
-            total = jnp.zeros((1, BLOCK), jnp.float32)
-            for tile, chosen in picks:
-                total += jnp.sum(
-                    jnp.where(chosen, jnp.exp(tile - top), 0.0), axis=0, keepdims=True
-                )
+            top, total, target_logit = block_stats(
+                project(q_all[block]), p_proj[...], meta[block], first_tile
+            )
 
             @pl.when(t == 0)
             def _():
@@ -252,15 +297,50 @@
 
     lax.fori_loop(0, 2 * n - 1, meet, 0)
 
+    if short:
+        @pl.when(folded & jnp.logical_not(outer))
+        def _():
+            pltpu.make_async_copy(p_far, p_far, pf_recv).wait()
+            held = project(p_far[...])
+            far_tile = beside * tiles + x * (rows_p // BLOCK)
+            for i in range(2):
+                if i == 1:
+                    for h in range(PIECES):
+                        view = q_far.at[pl.ds(h * piece_q, piece_q)]
+                        pltpu.make_async_copy(view, view, qf_recv.at[h]).wait()
+                    view = meta.at[n]
+                    pltpu.make_async_copy(view, view, mf_recv).wait()
+                rows = q_far[...] if i else q_all[far]
+                info = meta[n] if i else meta[far]
+                found = block_stats(project(rows), held, info, far_tile)
+                for j in range(3):
+                    far_out[i, j:j + 1, :] = found[j]
+                ex_copy(i).start()
+
+    def reaches(other):
+        ends = (z + other == n - 1) & outer
+        return jnp.logical_not(folded & ends) if short else other >= 0
+
     for o in range(1, n):
-        view = stats_in.at[lax.rem(z + o, n)]
-        pltpu.make_async_copy(view, view, st_recv.at[lax.rem(z + o, n)]).wait()
+        other = lax.rem(z + o, n)
+
+        @pl.when(reaches(other))
+        def _():
+            view = stats_in.at[other]
+            pltpu.make_async_copy(view, view, st_recv.at[other]).wait()
+
+    if short:
+        @pl.when(folded & outer)
+        def _():
+            for i in range(2):
+                view = stats_in.at[n + i]
+                pltpu.make_async_copy(view, view, ex_recv.at[i]).wait()
     top = stats_in[0, 0:1, :]
-    for i in range(1, n):
+    for i in range(1, slots):
         top = jnp.maximum(top, stats_in[i, 0:1, :])
     total = jnp.zeros((1, BLOCK), jnp.float32)
     target_logit = jnp.zeros((1, BLOCK), jnp.float32)
-    for i in range(n):
+    for i in range(slots):
         total += stats_in[i, 1:2, :] * jnp.exp(stats_in[i, 0:1, :] - top)
         target_logit += stats_in[i, 2:3, :]
     out_ref[...] = top + jnp.log(total) - target_logit
@@ -274,7 +354,23 @@
                 for h in range(PIECES):
                     q_copy(way, step, h).wait_send()
     for o in range(1, n):
-        stats_copy(lax.rem(z + o, n)).wait_send()
+        other = lax.rem(z + o, n)
+
+        @pl.when(reaches(other))
+        def _():
+            stats_copy(other).wait_send()
+    if short:
+        @pl.when(folded & outer)
+        def _():
+            pf_copy().wait_send()
+            mf_copy().wait_send()
+
+        @pl.when(folded & jnp.logical_not(outer))
+        def _():
+            for h in range(PIECES):
+                qf_copy(h).wait_send()
+            for i in range(2):
+                ex_copy(i).wait_send()
 
 
 def local(sizes, queries, passages, head_weight, positives, negative_ids, negative_count):
@@ -298,11 +394,14 @@
             pltpu.VMEM((pairs * rows_p, width), jnp.bfloat16),
             pltpu.VMEM((pairs * rows_p, width), jnp.bfloat16),
             pltpu.VMEM((shards * head_weight.shape[0], width), jnp.bfloat16),
-            pltpu.VMEM((n, meta_rows, BLOCK), jnp.int32),
+            pltpu.VMEM((n + 1, meta_rows, BLOCK), jnp.int32),
             pltpu.VMEM((n, 8, BLOCK), jnp.float32),
-            pltpu.VMEM((n, 8, BLOCK), jnp.float32),
+            pltpu.VMEM((n + 2, 8, BLOCK), jnp.float32),
             pltpu.SMEM(negative_ids.shape, jnp.int32),
             pltpu.SMEM(negative_count.shape, jnp.int32),
+            pltpu.VMEM((rows_p, width), jnp.bfloat16),
+            pltpu.VMEM((BLOCK, width), jnp.bfloat16),
+            pltpu.VMEM((2, 8, BLOCK), jnp.float32),
             dma((6,)),
             dma((2, hops, PIECES)), dma((2, hops, PIECES)),
             dma((max(pairs - 1, 1),)), dma((max(pairs - 1, 1),)),
@@ -311,6 +410,7 @@
             dma((far, PIECES)), dma((far, PIECES)),
             dma((hops,)), dma((hops,)),
             dma((n,)), dma((n,)),
+            dma, dma, dma((PIECES,)), dma((PIECES,)), dma, dma, dma((2,)), dma((2,)),
         ],
         compiler_params=pltpu.CompilerParams(
             collective_id=0, has_side_effects=True, vmem_limit_bytes=64 * 1024 * 1024

time: 30.8 us -> 32.7 us (1.062)
  the two profiles are of different devices: /device:TPU:0 before, /device:TPU:1 now
where the time goes in v3:
time: 32.7 us; the launch traced here: 32.6 us
  Pallas kernels  30.7 us (94%)
  local copies, waits for them, and re-layouts  1.19 us (4%)
  between operations  0.66 us (2%)
    pallas_call x1, Pallas kernels, local(): pl.pallas_call(functools.partial(kernel, sizes), out_shape=jax.ShapeDtype...  30.7 us
    unnamed x1, local copies, waits for them, and re-layouts  1.19 us

profile of v3, /device:TPU:1, one launch (start us, length us, event | category | flops | bytes accessed | tf_op | source)
XLA Modules:
  0.0 32.6 jit_solution(587935491072177425)
XLA Ops:
  0.7 30.7 %retriever_loss.1 = f32[1,128]{1,0:T(1,128)} custom-call(bf16[1,128,1024]{2,1,0:T(8,128)(2,1)} %q_ref.1, bf16[1,256,1024]{2,1,0:T(8,128)(2,1)} %p_ref.1, bf16[256,1024]{1,0:T(8,128)(2,1)} %w_ref.1, s32[1,128]{1,0:T(1,128)} %pos_ref.1, s32[1,1,2]{2,1,0:T(1,128)} %ids_ref.1, s32[1,1]{1,0:T(1,128)S(6)} %copy.8.count_ref), custom_call_target="tpu_custom_call" | custom-call | tf_op jit(solution)/shard_map/retriever_loss/pallas_call | solution.py:385
  31.4 1.2 %copy.9 = f32[1,128]{1,0:T(1,128)} copy(f32[1,128]{1,0:T(1,128)} %retriever_loss.1) | data formatting | bytes 1024

commit v4 on v2

--- a/solution.py
+++ b/solution.py
@@ -17,6 +17,7 @@
 def kernel(
     sizes, q_ref, p_ref, w_ref, pos_ref, ids_ref, count_ref, out_ref,
     q_all, p_all, p_proj, w_all, meta, stats_out, stats_in, ids_own, count_own,
+    p_part, q_part, q_proj,
     local_sem, q_send, q_recv, p_send, p_recv, own_send, own_recv,
     wy_send, wy_recv, wc_send, wc_recv, meta_send, meta_recv, st_send, st_recv,
 ):
@@ -27,6 +28,7 @@
     width = q_ref.shape[2]
     piece_q = BLOCK // PIECES
     piece_w = rows_w // PIECES
+    piece_p = rows_p // PIECES
     scale = width ** -0.5
     z = lax.axis_index("dp")
     f = lax.axis_index("fsdp")
@@ -43,6 +45,12 @@
     def shard_rows(shard, c):
         start = pl.multiple_of(shard * rows_w + c * piece_w, piece_w)
         return w_all.at[pl.ds(start, piece_w)]
+
+    def p_rows(holder, h):
+        return p_all.at[p_piece(holder, h)]
+
+    def p_piece(holder, h):
+        return pl.ds(pl.multiple_of(holder * rows_p + h * piece_p, piece_p), piece_p)
 
     own_w = w_all.at[pl.ds(pl.multiple_of(f * rows_w, rows_w), rows_w)]
     own_p = p_all.at[pl.ds(pl.multiple_of(x * rows_p, rows_p), rows_p)]
@@ -115,13 +123,14 @@
             )
             copy.start()
             sent.append(copy)
-    for o in range(1, pairs):
-        copy = remote(
-            p_ref.at[0], own_p, p_send.at[o - 1], p_recv.at[o - 1],
-            {"query": lax.rem(x + o, pairs)},
-        )
-        copy.start()
-        sent.append(copy)
+    for h in range(PIECES):
+        for o in range(1, pairs):
+            copy = remote(
+                p_ref.at[0, pl.ds(h * piece_p, piece_p)], p_rows(x, h),
+                p_send.at[o - 1, h], p_recv.at[o - 1, h], {"query": lax.rem(x + o, pairs)},
+            )
+            copy.start()
+            sent.append(copy)
     own_copy = remote(w_ref, own_w, own_send, own_recv, {"fsdp": mate})
     own_copy.start()
     sent.append(own_copy)
@@ -152,33 +161,89 @@
             copy.start()
             sent.append(copy)
 
-    events = [(step * PIECES + h, 0, (step, h)) for step in range(n - 2) for h in range(PIECES)]
-    events += [(2 * c + 1, 1, c) for c in range(PIECES)]
-    for _, kind, what in sorted(events):
-        if kind == 0:
-            pass_queries(*what)
-        else:
-            pass_weights(what)
-
+    def span(shard, c, depth):
+        return pl.ds(pl.multiple_of(shard * rows_w + c * piece_w, depth), depth)
+
+    fine = piece_w % 128 == 0
+    towers_from = [lax.rem(f - core + CORES * o, shards) for o in range(1, towers)]
+    first_spans = [span(f - core, 0, CORES * rows_w)]
+    if fine:
+        piece_spans = [
+            [span(base + k, c, piece_w) for base in towers_from for k in range(CORES)]
+            for c in range(PIECES)
+        ]
+        last_spans = [one for c in range(1, PIECES) for one in piece_spans[c]]
+    else:
+        last_spans = [span(base, 0, CORES * rows_w) for base in towers_from]
+
+    def partly(rows, spans):
+        lhs = [rows[:, one] for one in spans]
+        rhs = [w_all[one, :] for one in spans]
+        lhs = lhs[0] if len(lhs) == 1 else jnp.concatenate(lhs, axis=1)
+        rhs = rhs[0] if len(rhs) == 1 else jnp.concatenate(rhs, axis=0)
+        return jnp.dot(lhs, rhs, preferred_element_type=jnp.float32)
+
+    def project(rows):
+        return jnp.dot(rows, w_all[...], preferred_element_type=jnp.float32).astype(jnp.bfloat16)
+
+    def mate_weights(c):
+        for o in range(1, towers):
+            view = shard_rows(lax.rem(mate + shards - CORES * o, shards), c)
+            pltpu.make_async_copy(view, view, wc_recv.at[o - 1, c]).wait()
+
+    def neighbours(act):
+        for way in range(2):
+            @pl.when(q_receives(way, 0))
+            def _():
+                act(q_all.at[z - 1 if way == 0 else z + 1], q_part.at[1 + way])
+
+    def begin(rows, part):
+        part[...] = partly(rows, first_spans)
+
+    def extend(rows, part):
+        part[...] += partly(rows, piece_spans[0])
+
+    own_part = p_part.at[pl.ds(pl.multiple_of(x * rows_p, rows_p), rows_p)]
     for copy in locals_:
         copy.wait()
     other_w = w_all.at[pl.ds(pl.multiple_of(mate * rows_w, rows_w), rows_w)]
     pltpu.make_async_copy(other_w, other_w, own_recv).wait()
-    for c in range(PIECES):
-        for o in range(1, towers):
-            view = shard_rows(lax.rem(mate + shards - CORES * o, shards), c)
-            pltpu.make_async_copy(view, view, wc_recv.at[o - 1, c]).wait()
-
-    def project(rows):
-        return jnp.dot(rows, w_all[...], preferred_element_type=jnp.float32).astype(jnp.bfloat16)
+    begin(own_p, own_part)
+    begin(q_all.at[z], q_part.at[0])
+    pass_queries(0, 0)
+    pass_weights(0)
+    pass_queries(0, 1)
+    neighbours(begin)
+    mate_weights(0)
+    if fine:
+        extend(own_p, own_part)
+        extend(q_all.at[z], q_part.at[0])
+        neighbours(extend)
+    for o in range(1, pairs):
+        holder = lax.rem(x + pairs - o, pairs)
+        view = p_rows(holder, 0)
+        pltpu.make_async_copy(view, view, p_recv.at[o - 1, 0]).wait()
+        p_part[p_piece(holder, 0), :] = partly(
+            view, first_spans + piece_spans[0] if fine else first_spans
+        )
+    for step in range(1, n - 2):
+        pass_queries(step, 0)
+        if step == 1:
+            pass_weights(1)
+        pass_queries(step, 1)
+    mate_weights(1)
 
     for o in range(pairs):
         holder = lax.rem(x + pairs - o, pairs)
-        part = pl.ds(pl.multiple_of(holder * rows_p, rows_p), rows_p)
-        if o:
-            view = p_all.at[part]
-            pltpu.make_async_copy(view, view, p_recv.at[o - 1]).wait()
-        p_proj[part, :] = project(p_all[part, :])
+        for h in range(PIECES):
+            view = p_rows(holder, h)
+            piece = p_piece(holder, h)
+            if o and h:
+                pltpu.make_async_copy(view, view, p_recv.at[o - 1, h]).wait()
+                p_proj[piece, :] = project(view[...])
+            else:
+                whole = p_part[piece, :] + partly(view, last_spans)
+                p_proj[piece, :] = whole.astype(jnp.bfloat16)
 
     for o in range(1, n):
         view = meta.at[lax.rem(z + n - o, n)]
@@ -201,15 +266,25 @@
 
         @pl.when((place >= 0) & (place < n))
         def _():
+            @pl.when(away <= 1)
+            def _():
+                rest = partly(q_all.at[block], last_spans)
+                q_proj[...] = (q_part[jnp.minimum(t, 2)] + rest).astype(jnp.bfloat16)
+
+            @pl.when((away > 1) & (away < n - 1))
+            def _():
+                q_proj[...] = project(q_all[block])
+
             @pl.when(away == n - 1)
             def _():
                 for h in range(PIECES):
-                    view = q_all.at[block, pl.ds(h * piece_q, piece_q)]
+                    part = pl.ds(h * piece_q, piece_q)
+                    view = q_all.at[block, part]
                     pltpu.make_async_copy(view, view, q_recv.at[way, n - 2, h]).wait()
-
-            q_proj = project(q_all[block])
+                    q_proj[part, :] = project(view[...])
+
             logits = lax.dot_general(
-                p_proj[...], q_proj, (((1,), (1,)), ((), ())),
+                p_proj[...], q_proj[...], (((1,), (1,)), ((), ())),
                 preferred_element_type=jnp.float32,
             ) * scale
             info = meta[block]
@@ -303,9 +378,12 @@
             pltpu.VMEM((n, 8, BLOCK), jnp.float32),
             pltpu.SMEM(negative_ids.shape, jnp.int32),
             pltpu.SMEM(negative_count.shape, jnp.int32),
+            pltpu.VMEM((pairs * rows_p, width), jnp.float32),
+            pltpu.VMEM((3, BLOCK, width), jnp.float32),
+            pltpu.VMEM((BLOCK, width), jnp.bfloat16),
             dma((6,)),
             dma((2, hops, PIECES)), dma((2, hops, PIECES)),
-            dma((max(pairs - 1, 1),)), dma((max(pairs - 1, 1),)),
+            dma((max(pairs - 1, 1), PIECES)), dma((max(pairs - 1, 1), PIECES)),
             dma, dma,
             dma((far, PIECES)), dma((far, PIECES)),
             dma((far, PIECES)), dma((far, PIECES)),

time: 30.8 us -> 31.1 us (level)
  Pallas kernels: 28.5 us -> 29 us
    pallas_call x1, Pallas kernels: 28.5 us -> 29 us  [local(): pl.pallas_call(functools.partial(kernel, sizes), out_shape=jax.ShapeDtype...]
where the time goes in v4:
time: 31.1 us; the launch traced here: 30.9 us
  Pallas kernels  29 us (93%)
  local copies, waits for them, and re-layouts  1.19 us (4%)
  between operations  0.66 us (2%)
    pallas_call x1, Pallas kernels, local(): pl.pallas_call(functools.partial(kernel, sizes), out_shape=jax.ShapeDtype...  29 us
    unnamed x1, local copies, waits for them, and re-layouts  1.19 us

profile of v4, /device:TPU:0, one launch (start us, length us, event | category | flops | bytes accessed | tf_op | source)
XLA Modules:
  0.0 30.9 jit_solution(4783428588493085719)
XLA Ops:
  0.7 29.0 %retriever_loss.1 = f32[1,128]{1,0:T(1,128)} custom-call(bf16[1,128,1024]{2,1,0:T(8,128)(2,1)} %q_ref.1, bf16[1,256,1024]{2,1,0:T(8,128)(2,1)} %p_ref.1, bf16[256,1024]{1,0:T(8,128)(2,1)} %w_ref.1, s32[1,128]{1,0:T(1,128)} %pos_ref.1, s32[1,1,2]{2,1,0:T(1,128)} %ids_ref.1, s32[1,1]{1,0:T(1,128)S(6)} %copy.8.count_ref), custom_call_target="tpu_custom_call" | custom-call | tf_op jit(solution)/shard_map/retriever_loss/pallas_call | solution.py:364
  29.7 1.2 %copy.9 = f32[1,128]{1,0:T(1,128)} copy(f32[1,128]{1,0:T(1,128)} %retriever_loss.1) | data formatting | bytes 1024

commit v5 on v4

--- a/solution.py
+++ b/solution.py
@@ -17,9 +17,10 @@
 def kernel(
     sizes, q_ref, p_ref, w_ref, pos_ref, ids_ref, count_ref, out_ref,
     q_all, p_all, p_proj, w_all, meta, stats_out, stats_in, ids_own, count_own,
-    p_part, q_part, q_proj,
+    p_part, q_part, q_proj, p_far, q_far, far_out,
     local_sem, q_send, q_recv, p_send, p_recv, own_send, own_recv,
     wy_send, wy_recv, wc_send, wc_recv, meta_send, meta_recv, st_send, st_recv,
+    pf_send, pf_recv, qf_send, qf_recv, mf_send, mf_recv, ex_send, ex_recv,
 ):
     n, shards, pairs, max_list = sizes
     towers = shards // CORES
@@ -35,6 +36,14 @@
     x = lax.axis_index("query")
     core = lax.rem(f, CORES)
     mate = f + 1 - 2 * core
+
+    short = n == 4 and pairs == 2
+    folded = (core == 1) if short else False
+    outer = (z == 0) | (z == n - 1)
+    far = lax.rem(z + 2, n)
+    beside = z + 1 - 2 * lax.rem(z, 2)
+    across = lax.rem(x + 1, pairs)
+    slots = n + 2 if short else n
 
     def remote(src, dst, send, recv, where):
         return pltpu.make_async_remote_copy(
@@ -74,6 +83,11 @@
     friends += [{"query": lax.rem(x + o, pairs)} for o in range(1, pairs)]
     friends += [{"fsdp": lax.rem(f + CORES * o, shards)} for o in range(1, towers)]
     friends += [{"fsdp": mate}]
+    if short:
+        friends += [{"dp": far, "query": across}]
+    for i in range(slots):
+        stats_in[i, 0:1, :] = jnp.full((1, BLOCK), MASKED, jnp.float32)
+        stats_in[i, 1:3, :] = jnp.zeros((2, BLOCK), jnp.float32)
     for friend in friends:
         pl.semaphore_signal(barrier, inc=1, device_id=friend, device_id_type=MESH)
 
@@ -94,9 +108,8 @@
         return remote(src, view, q_send.at[way, step, h], q_recv.at[way, step, h], {"dp": target})
 
     def q_sends(way, step):
-        if way == 0:
-            return (z + 1 < n) & (z >= step)
-        return (z >= 1) & (z + step < n)
+        there = (z + 1 < n) & (z >= step) if way == 0 else (z >= 1) & (z + step < n)
+        return there & jnp.logical_not(folded) if short and step == n - 2 else there
 
     def q_wait(way, step, h):
         block = z - 1 - step if way == 0 else z + 1 + step
@@ -106,6 +119,22 @@
 
     def q_receives(way, step):
         return z - 1 - step >= 0 if way == 0 else z + 1 + step < n
+
+    def qf_copy(h):
+        part = pl.ds(h * piece_q, piece_q)
+        return remote(
+            q_all.at[far, part], q_far.at[part], qf_send.at[h], qf_recv.at[h], {"query": across}
+        )
+
+    def pf_copy():
+        return remote(p_ref.at[0], p_far, pf_send, pf_recv, {"dp": beside})
+
+    def mf_copy():
+        return remote(meta.at[z], meta.at[n], mf_send, mf_recv, {"dp": far, "query": across})
+
+    def ex_copy(i):
+        where = {"dp": far, "query": across} if i else {"dp": far}
+        return remote(far_out.at[i], stats_in.at[n + i], ex_send.at[i], ex_recv.at[i], where)
 
     for h in range(PIECES):
         for way in range(2):
@@ -131,6 +160,11 @@
             )
             copy.start()
             sent.append(copy)
+    if short:
+        @pl.when(folded & outer)
+        def _():
+            pf_copy().start()
+            mf_copy().start()
     own_copy = remote(w_ref, own_w, own_send, own_recv, {"fsdp": mate})
     own_copy.start()
     sent.append(own_copy)
@@ -151,6 +185,11 @@
             @pl.when(q_sends(way, step + 1))
             def _():
                 q_copy(way, step + 1, h).start()
+
+        if short and step == 1:
+            @pl.when(folded & jnp.logical_not(outer))
+            def _():
+                qf_copy(h).start()
 
     def pass_weights(c):
         for o in range(1, towers):
@@ -258,13 +297,54 @@
             stats_out.at[block], stats_in.at[z], st_send.at[block], st_recv.at[z], {"dp": block}
         )
 
+    def block_stats(held, info, tile_id):
+        logits = lax.dot_general(
+            held, q_proj[...], (((1,), (1,)), ((), ())), preferred_element_type=jnp.float32
+        ) * scale
+        target = info[0:1, :]
+        top = jnp.full((1, BLOCK), MASKED, jnp.float32)
+        target_logit = jnp.zeros((1, BLOCK), jnp.float32)
+        picks = []
+        for k in range(held.shape[0] // BLOCK):
+            tile = logits[k * BLOCK:(k + 1) * BLOCK, :]
+            listed = info[1:2, :] == tile_id + k
+            for l in range(1, max_list):
+                listed = listed | (info[l + 1:l + 2, :] == tile_id + k)
+            is_target = row_index == target - (tile_id + k) * BLOCK
+            chosen = listed | is_target
+            picks.append((tile, chosen))
+            top = jnp.maximum(
+                top, jnp.max(jnp.where(chosen, tile, MASKED), axis=0, keepdims=True)
+            )
+            target_logit += jnp.sum(jnp.where(is_target, tile, 0.0), axis=0, keepdims=True)
+        total = jnp.zeros((1, BLOCK), jnp.float32)
+        for tile, chosen in picks:
+            total += jnp.sum(jnp.where(chosen, jnp.exp(tile - top), 0.0), axis=0, keepdims=True)
+        return top, total, target_logit
+
+    def far_stats(i, info):
+        found = block_stats(p_far[...], info, beside * tiles + x * (rows_p // BLOCK))
+        for j in range(3):
+            far_out[i, j:j + 1, :] = found[j]
+        ex_copy(i).start()
+
+    if short:
+        @pl.when(folded & jnp.logical_not(outer))
+        def _():
+            pltpu.make_async_copy(p_far, p_far, pf_recv).wait()
+            p_far[...] = project(p_far[...])
+
     def meet(t, carry):
         away = lax.div(t + 1, 2)
         way = lax.rem(t + 1, 2)
         place = jnp.where(way == 0, z - away, z + away)
         block = jnp.clip(place, 0, n - 1)
 
-        @pl.when((place >= 0) & (place < n))
+        meets = (place >= 0) & (place < n)
+        if short:
+            meets = meets & jnp.logical_not(folded & (away == n - 1))
+
+        @pl.when(meets)
         def _():
             @pl.when(away <= 1)
             def _():
@@ -283,32 +363,7 @@
                     pltpu.make_async_copy(view, view, q_recv.at[way, n - 2, h]).wait()
                     q_proj[part, :] = project(view[...])
 
-            logits = lax.dot_general(
-                p_proj[...], q_proj[...], (((1,), (1,)), ((), ())),
-                preferred_element_type=jnp.float32,
-            ) * scale
-            info = meta[block]
-            target = info[0:1, :]
-            top = jnp.full((1, BLOCK), MASKED, jnp.float32)
-            target_logit = jnp.zeros((1, BLOCK), jnp.float32)
-            picks = []
-            for k in range(tiles):
-                tile = logits[k * BLOCK:(k + 1) * BLOCK, :]
-                listed = info[1:2, :] == first_tile + k
-                for l in range(1, max_list):
-                    listed = listed | (info[l + 1:l + 2, :] == first_tile + k)
-                is_target = row_index == target - (first_tile + k) * BLOCK
-                chosen = listed | is_target
-                picks.append((tile, chosen))
-                top = jnp.maximum(
-                    top, jnp.max(jnp.where(chosen, tile, MASKED), axis=0, keepdims=True)
-                )
-                target_logit += jnp.sum(jnp.where(is_target, tile, 0.0), axis=0, keepdims=True)
-            total = jnp.zeros((1, BLOCK), jnp.float32)
-            for tile, chosen in picks:
-                total += jnp.sum(
-                    jnp.where(chosen, jnp.exp(tile - top), 0.0), axis=0, keepdims=True
-                )
+            top, total, target_logit = block_stats(p_proj[...], meta[block], first_tile)
 
             @pl.when(t == 0)
             def _():
@@ -323,19 +378,50 @@
                 stats_out[block, 2:3, :] = target_logit
                 stats_copy(block).start()
 
+            if short:
+                @pl.when(folded & jnp.logical_not(outer) & (away == 2))
+                def _():
+                    far_stats(0, meta[block])
+
         return carry
 
     lax.fori_loop(0, 2 * n - 1, meet, 0)
 
+    if short:
+        @pl.when(folded & jnp.logical_not(outer))
+        def _():
+            for h in range(PIECES):
+                view = q_far.at[pl.ds(h * piece_q, piece_q)]
+                pltpu.make_async_copy(view, view, qf_recv.at[h]).wait()
+            view = meta.at[n]
+            pltpu.make_async_copy(view, view, mf_recv).wait()
+            q_proj[...] = project(q_far[...])
+            far_stats(1, meta[n])
+
+    def reaches(other):
+        ends = (z + other == n - 1) & outer
+        return jnp.logical_not(folded & ends) if short else other >= 0
+
     for o in range(1, n):
-        view = stats_in.at[lax.rem(z + o, n)]
-        pltpu.make_async_copy(view, view, st_recv.at[lax.rem(z + o, n)]).wait()
+        other = lax.rem(z + o, n)
+
+        @pl.when(reaches(other))
+        def _():
+            view = stats_in.at[other]
+            pltpu.make_async_copy(view, view, st_recv.at[other]).wait()
+
+    if short:
+        @pl.when(folded & outer)
+        def _():
+            for i in range(2):
+                view = stats_in.at[n + i]
+                pltpu.make_async_copy(view, view, ex_recv.at[i]).wait()
     top = stats_in[0, 0:1, :]
-    for i in range(1, n):
+    for i in range(1, slots):
         top = jnp.maximum(top, stats_in[i, 0:1, :])
     total = jnp.zeros((1, BLOCK), jnp.float32)
     target_logit = jnp.zeros((1, BLOCK), jnp.float32)
-    for i in range(n):
+    for i in range(slots):
         total += stats_in[i, 1:2, :] * jnp.exp(stats_in[i, 0:1, :] - top)
         target_logit += stats_in[i, 2:3, :]
     out_ref[...] = top + jnp.log(total) - target_logit
@@ -349,7 +435,23 @@
                 for h in range(PIECES):
                     q_copy(way, step, h).wait_send()
     for o in range(1, n):
-        stats_copy(lax.rem(z + o, n)).wait_send()
+        other = lax.rem(z + o, n)
+
+        @pl.when(reaches(other))
+        def _():
+            stats_copy(other).wait_send()
+    if short:
+        @pl.when(folded & outer)
+        def _():
+            pf_copy().wait_send()
+            mf_copy().wait_send()
+
+        @pl.when(folded & jnp.logical_not(outer))
+        def _():
+            for h in range(PIECES):
+                qf_copy(h).wait_send()
+            for i in range(2):
+                ex_copy(i).wait_send()
 
 
 def local(sizes, queries, passages, head_weight, positives, negative_ids, negative_count):
@@ -373,14 +475,17 @@
             pltpu.VMEM((pairs * rows_p, width), jnp.bfloat16),
             pltpu.VMEM((pairs * rows_p, width), jnp.bfloat16),
             pltpu.VMEM((shards * head_weight.shape[0], width), jnp.bfloat16),
-            pltpu.VMEM((n, meta_rows, BLOCK), jnp.int32),
+            pltpu.VMEM((n + 1, meta_rows, BLOCK), jnp.int32),
             pltpu.VMEM((n, 8, BLOCK), jnp.float32),
-            pltpu.VMEM((n, 8, BLOCK), jnp.float32),
+            pltpu.VMEM((n + 2, 8, BLOCK), jnp.float32),
             pltpu.SMEM(negative_ids.shape, jnp.int32),
             pltpu.SMEM(negative_count.shape, jnp.int32),
             pltpu.VMEM((pairs * rows_p, width), jnp.float32),
             pltpu.VMEM((3, BLOCK, width), jnp.float32),
             pltpu.VMEM((BLOCK, width), jnp.bfloat16),
+            pltpu.VMEM((rows_p, width), jnp.bfloat16),
+            pltpu.VMEM((BLOCK, width), jnp.bfloat16),
+            pltpu.VMEM((2, 8, BLOCK), jnp.float32),
             dma((6,)),
             dma((2, hops, PIECES)), dma((2, hops, PIECES)),
             dma((max(pairs - 1, 1), PIECES)), dma((max(pairs - 1, 1), PIECES)),
@@ -389,6 +494,7 @@
             dma((far, PIECES)), dma((far, PIECES)),
             dma((hops,)), dma((hops,)),
             dma((n,)), dma((n,)),
+            dma, dma, dma((PIECES,)), dma((PIECES,)), dma, dma, dma((2,)), dma((2,)),
         ],
         compiler_params=pltpu.CompilerParams(
             collective_id=0, has_side_effects=True, vmem_limit_bytes=64 * 1024 * 1024

time: 31.1 us -> 31.2 us (level)
  the two profiles are of different devices: /device:TPU:0 before, /device:TPU:1 now
where the time goes in v5:
time: 31.2 us; the launch traced here: 31 us
  Pallas kernels  29.2 us (94%)
  local copies, waits for them, and re-layouts  1.19 us (4%)
  between operations  0.66 us (2%)
    pallas_call x1, Pallas kernels, local(): pl.pallas_call(functools.partial(kernel, sizes), out_shape=jax.ShapeDtype...  29.2 us
    unnamed x1, local copies, waits for them, and re-layouts  1.19 us

profile of v5, /device:TPU:1, one launch (start us, length us, event | category | flops | bytes accessed | tf_op | source)
XLA Modules:
  0.0 31.0 jit_solution(17910109020560968012)
XLA Ops:
  0.7 29.2 %retriever_loss.1 = f32[1,128]{1,0:T(1,128)} custom-call(bf16[1,128,1024]{2,1,0:T(8,128)(2,1)} %q_ref.1, bf16[1,256,1024]{2,1,0:T(8,128)(2,1)} %p_ref.1, bf16[256,1024]{1,0:T(8,128)(2,1)} %w_ref.1, s32[1,128]{1,0:T(1,128)} %pos_ref.1, s32[1,1,2]{2,1,0:T(1,128)} %ids_ref.1, s32[1,1]{1,0:T(1,128)S(6)} %copy.8.count_ref), custom_call_target="tpu_custom_call" | custom-call | tf_op jit(solution)/shard_map/retriever_loss/pallas_call | solution.py:466
  29.9 1.2 %copy.9 = f32[1,128]{1,0:T(1,128)} copy(f32[1,128]{1,0:T(1,128)} %retriever_loss.1) | data formatting | bytes 1024

commit v6 on v4

--- a/solution.py
+++ b/solution.py
@@ -164,17 +164,9 @@
     def span(shard, c, depth):
         return pl.ds(pl.multiple_of(shard * rows_w + c * piece_w, depth), depth)
 
-    fine = piece_w % 128 == 0
     towers_from = [lax.rem(f - core + CORES * o, shards) for o in range(1, towers)]
     first_spans = [span(f - core, 0, CORES * rows_w)]
-    if fine:
-        piece_spans = [
-            [span(base + k, c, piece_w) for base in towers_from for k in range(CORES)]
-            for c in range(PIECES)
-        ]
-        last_spans = [one for c in range(1, PIECES) for one in piece_spans[c]]
-    else:
-        last_spans = [span(base, 0, CORES * rows_w) for base in towers_from]
+    last_spans = [span(base, 0, CORES * rows_w) for base in towers_from]
 
     def partly(rows, spans):
         lhs = [rows[:, one] for one in spans]
@@ -199,9 +191,6 @@
 
     def begin(rows, part):
         part[...] = partly(rows, first_spans)
-
-    def extend(rows, part):
-        part[...] += partly(rows, piece_spans[0])
 
     own_part = p_part.at[pl.ds(pl.multiple_of(x * rows_p, rows_p), rows_p)]
     for copy in locals_:
@@ -211,26 +200,15 @@
     begin(own_p, own_part)
     begin(q_all.at[z], q_part.at[0])
     pass_queries(0, 0)
-    pass_weights(0)
     pass_queries(0, 1)
     neighbours(begin)
-    mate_weights(0)
-    if fine:
-        extend(own_p, own_part)
-        extend(q_all.at[z], q_part.at[0])
-        neighbours(extend)
-    for o in range(1, pairs):
-        holder = lax.rem(x + pairs - o, pairs)
-        view = p_rows(holder, 0)
-        pltpu.make_async_copy(view, view, p_recv.at[o - 1, 0]).wait()
-        p_part[p_piece(holder, 0), :] = partly(
-            view, first_spans + piece_spans[0] if fine else first_spans
-        )
     for step in range(1, n - 2):
         pass_queries(step, 0)
         if step == 1:
-            pass_weights(1)
+            pass_weights(0)
         pass_queries(step, 1)
+    pass_weights(1)
+    mate_weights(0)
     mate_weights(1)
 
     for o in range(pairs):
@@ -238,7 +216,7 @@
         for h in range(PIECES):
             view = p_rows(holder, h)
             piece = p_piece(holder, h)
-            if o and h:
+            if o:
                 pltpu.make_async_copy(view, view, p_recv.at[o - 1, h]).wait()
                 p_proj[piece, :] = project(view[...])
             else:

time: 31.1 us -> 31.1 us (level)
  no operation moved by 1% of the time
where the time goes in v6:
time: 31.1 us; the launch traced here: 30.8 us
  Pallas kernels  28.9 us (93%)
  local copies, waits for them, and re-layouts  1.19 us (4%)
  between operations  0.66 us (2%)
    pallas_call x1, Pallas kernels, local(): pl.pallas_call(functools.partial(kernel, sizes), out_shape=jax.ShapeDtype...  28.9 us
    unnamed x1, local copies, waits for them, and re-layouts  1.19 us

profile of v6, /device:TPU:0, one launch (start us, length us, event | category | flops | bytes accessed | tf_op | source)
XLA Modules:
  0.0 30.8 jit_solution(7306647301469225971)
XLA Ops:
  0.7 28.9 %retriever_loss.1 = f32[1,128]{1,0:T(1,128)} custom-call(bf16[1,128,1024]{2,1,0:T(8,128)(2,1)} %q_ref.1, bf16[1,256,1024]{2,1,0:T(8,128)(2,1)} %p_ref.1, bf16[256,1024]{1,0:T(8,128)(2,1)} %w_ref.1, s32[1,128]{1,0:T(1,128)} %pos_ref.1, s32[1,1,2]{2,1,0:T(1,128)} %ids_ref.1, s32[1,1]{1,0:T(1,128)S(6)} %copy.8.count_ref), custom_call_target="tpu_custom_call" | custom-call | tf_op jit(solution)/shard_map/retriever_loss/pallas_call | solution.py:342
  29.6 1.2 %copy.9 = f32[1,128]{1,0:T(1,128)} copy(f32[1,128]{1,0:T(1,128)} %retriever_loss.1) | data formatting | bytes 1024

commit v7 on v4

--- a/solution.py
+++ b/solution.py
@@ -85,7 +85,15 @@
         meta[z, l + 1:l + 2, :] = jnp.full((1, BLOCK), entry, jnp.int32)
     pl.semaphore_wait(barrier, len(friends))
 
+    short = n == 4
+
     def q_copy(way, step, h):
+        if short and step == n - 2:
+            part = pl.ds(h * piece_q, piece_q)
+            return remote(
+                q_ref.at[0, part], q_all.at[z, part],
+                q_send.at[way, step, h], q_recv.at[way, step, h], {"dp": (n - 1) - z},
+            )
         block = z - step if way == 0 else z + step
         block = jnp.clip(block, 0, n - 1)
         view = q_all.at[block, pl.ds(h * piece_q, piece_q)]
@@ -94,6 +102,8 @@
         return remote(src, view, q_send.at[way, step, h], q_recv.at[way, step, h], {"dp": target})
 
     def q_sends(way, step):
+        if short and step == n - 2:
+            return z == 0 if way == 0 else z == n - 1
         if way == 0:
             return (z + 1 < n) & (z >= step)
         return (z >= 1) & (z + step < n)
@@ -131,6 +141,12 @@
             )
             copy.start()
             sent.append(copy)
+    if short:
+        for h in range(PIECES):
+            for way in range(2):
+                @pl.when(q_sends(way, n - 2))
+                def _():
+                    q_copy(way, n - 2, h).start()
     own_copy = remote(w_ref, own_w, own_send, own_recv, {"fsdp": mate})
     own_copy.start()
     sent.append(own_copy)
@@ -148,9 +164,10 @@
             def _():
                 q_wait(way, step, h)
 
-            @pl.when(q_sends(way, step + 1))
-            def _():
-                q_copy(way, step + 1, h).start()
+            if not (short and step + 1 == n - 2):
+                @pl.when(q_sends(way, step + 1))
+                def _():
+                    q_copy(way, step + 1, h).start()
 
     def pass_weights(c):
         for o in range(1, towers):

time: 31.1 us -> 34.6 us (1.11)
  Pallas kernels: 29 us -> 32.6 us
    pallas_call x1, Pallas kernels: 29 us -> 32.6 us  [local(): pl.pallas_call(functools.partial(kernel, sizes), out_shape=jax.ShapeDtype...]
where the time goes in v7:
time: 34.6 us; the launch traced here: 34.4 us
  Pallas kernels  32.6 us (94%)
  local copies, waits for them, and re-layouts  1.19 us (3%)
  between operations  0.66 us (2%)
    pallas_call x1, Pallas kernels, local(): pl.pallas_call(functools.partial(kernel, sizes), out_shape=jax.ShapeDtype...  32.6 us
    unnamed x1, local copies, waits for them, and re-layouts  1.19 us

profile of v7, /device:TPU:0, one launch (start us, length us, event | category | flops | bytes accessed | tf_op | source)
XLA Modules:
  0.0 34.4 jit_solution(1745811779286677194)
XLA Ops:
  0.7 32.6 %retriever_loss.1 = f32[1,128]{1,0:T(1,128)} custom-call(bf16[1,128,1024]{2,1,0:T(8,128)(2,1)} %q_ref.1, bf16[1,256,1024]{2,1,0:T(8,128)(2,1)} %p_ref.1, bf16[256,1024]{1,0:T(8,128)(2,1)} %w_ref.1, s32[1,128]{1,0:T(1,128)} %pos_ref.1, s32[1,1,2]{2,1,0:T(1,128)} %ids_ref.1, s32[1,1]{1,0:T(1,128)S(6)} %copy.8.count_ref), custom_call_target="tpu_custom_call" | custom-call | tf_op jit(solution)/shard_map/retriever_loss/pallas_call | solution.py:381
  33.2 1.2 %copy.9 = f32[1,128]{1,0:T(1,128)} copy(f32[1,128]{1,0:T(1,128)} %retriever_loss.1) | data formatting | bytes 1024

commit v8 on v4

--- a/solution.py
+++ b/solution.py
@@ -10,6 +10,7 @@
 BLOCK = 128
 CORES = 2
 PIECES = 2
+QUERY_PIECES = 4
 MASKED = -1e30
 MESH = pl.DeviceIdType.MESH
 
@@ -26,7 +27,7 @@
     rows_w = w_ref.shape[0]
     rows_p = p_ref.shape[1]
     width = q_ref.shape[2]
-    piece_q = BLOCK // PIECES
+    piece_q = BLOCK // QUERY_PIECES
     piece_w = rows_w // PIECES
     piece_p = rows_p // PIECES
     scale = width ** -0.5
@@ -107,7 +108,7 @@
     def q_receives(way, step):
         return z - 1 - step >= 0 if way == 0 else z + 1 + step < n
 
-    for h in range(PIECES):
+    for h in range(QUERY_PIECES):
         for way in range(2):
             @pl.when(q_sends(way, 0))
             def _():
@@ -210,9 +211,9 @@
     pltpu.make_async_copy(other_w, other_w, own_recv).wait()
     begin(own_p, own_part)
     begin(q_all.at[z], q_part.at[0])
-    pass_queries(0, 0)
+    for h in range(QUERY_PIECES):
+        pass_queries(0, h)
     pass_weights(0)
-    pass_queries(0, 1)
     neighbours(begin)
     mate_weights(0)
     if fine:
@@ -227,10 +228,10 @@
             view, first_spans + piece_spans[0] if fine else first_spans
         )
     for step in range(1, n - 2):
-        pass_queries(step, 0)
-        if step == 1:
-            pass_weights(1)
-        pass_queries(step, 1)
+        for h in range(QUERY_PIECES):
+            if step == 1 and h == QUERY_PIECES - 1:
+                pass_weights(1)
+            pass_queries(step, h)
     mate_weights(1)
 
     for o in range(pairs):
@@ -277,11 +278,12 @@
 
             @pl.when(away == n - 1)
             def _():
-                for h in range(PIECES):
-                    part = pl.ds(h * piece_q, piece_q)
-                    view = q_all.at[block, part]
+                for h in range(QUERY_PIECES):
+                    view = q_all.at[block, pl.ds(h * piece_q, piece_q)]
                     pltpu.make_async_copy(view, view, q_recv.at[way, n - 2, h]).wait()
-                    q_proj[part, :] = project(view[...])
+                    if h % 2:
+                        part = pl.ds((h - 1) * piece_q, 2 * piece_q)
+                        q_proj[part, :] = project(q_all[block, part])
 
             logits = lax.dot_general(
                 p_proj[...], q_proj[...], (((1,), (1,)), ((), ())),
@@ -346,7 +348,7 @@
         for way in range(2):
             @pl.when(q_sends(way, step))
             def _():
-                for h in range(PIECES):
+                for h in range(QUERY_PIECES):
                     q_copy(way, step, h).wait_send()
     for o in range(1, n):
         stats_copy(lax.rem(z + o, n)).wait_send()
@@ -382,7 +384,7 @@
             pltpu.VMEM((3, BLOCK, width), jnp.float32),
             pltpu.VMEM((BLOCK, width), jnp.bfloat16),
             dma((6,)),
-            dma((2, hops, PIECES)), dma((2, hops, PIECES)),
+            dma((2, hops, QUERY_PIECES)), dma((2, hops, QUERY_PIECES)),
             dma((max(pairs - 1, 1), PIECES)), dma((max(pairs - 1, 1), PIECES)),
             dma, dma,
             dma((far, PIECES)), dma((far, PIECES)),

time: 31.1 us -> 31 us (level)
  no operation moved by 1% of the time
where the time goes in v8:
time: 31 us; the launch traced here: 30.8 us
  Pallas kernels  29 us (94%)
  local copies, waits for them, and re-layouts  1.19 us (4%)
  between operations  0.66 us (2%)
    pallas_call x1, Pallas kernels, local(): pl.pallas_call(functools.partial(kernel, sizes), out_shape=jax.ShapeDtype...  29 us
    unnamed x1, local copies, waits for them, and re-layouts  1.19 us

profile of v8, /device:TPU:0, one launch (start us, length us, event | category | flops | bytes accessed | tf_op | source)
XLA Modules:
  0.0 30.8 jit_solution(12399179227163068213)
XLA Ops:
  0.7 29.0 %retriever_loss.1 = f32[1,128]{1,0:T(1,128)} custom-call(bf16[1,128,1024]{2,1,0:T(8,128)(2,1)} %q_ref.1, bf16[1,256,1024]{2,1,0:T(8,128)(2,1)} %p_ref.1, bf16[256,1024]{1,0:T(8,128)(2,1)} %w_ref.1, s32[1,128]{1,0:T(1,128)} %pos_ref.1, s32[1,1,2]{2,1,0:T(1,128)} %ids_ref.1, s32[1,1]{1,0:T(1,128)S(6)} %copy.8.count_ref), custom_call_target="tpu_custom_call" | custom-call | tf_op jit(solution)/shard_map/retriever_loss/pallas_call | solution.py:366
  29.6 1.2 %copy.9 = f32[1,128]{1,0:T(1,128)} copy(f32[1,128]{1,0:T(1,128)} %retriever_loss.1) | data formatting | bytes 1024

commit v9 on v8

--- a/solution.py
+++ b/solution.py
@@ -144,14 +144,17 @@
         sent.append(copy)
 
     def pass_queries(step, h):
-        for way in range(2):
-            @pl.when(q_receives(way, step))
-            def _():
-                q_wait(way, step, h)
-
-            @pl.when(q_sends(way, step + 1))
-            def _():
-                q_copy(way, step + 1, h).start()
+        for near in range(2):
+            for way in (1 - near, near):
+                side = z < n // 2 if near == 0 else z >= n // 2
+
+                @pl.when(side & q_receives(way, step))
+                def _():
+                    q_wait(way, step, h)
+
+                @pl.when(side & q_sends(way, step + 1))
+                def _():
+                    q_copy(way, step + 1, h).start()
 
     def pass_weights(c):
         for o in range(1, towers):

time: 31 us -> 31 us (level)
  no operation moved by 1% of the time
where the time goes in v9:
time: 31 us; the launch traced here: 30.9 us
  Pallas kernels  29 us (94%)
  local copies, waits for them, and re-layouts  1.19 us (4%)
  between operations  0.66 us (2%)
    pallas_call x1, Pallas kernels, local(): pl.pallas_call(functools.partial(kernel, sizes), out_shape=jax.ShapeDtype...  29 us
    unnamed x1, local copies, waits for them, and re-layouts  1.19 us

profile of v9, /device:TPU:0, one launch (start us, length us, event | category | flops | bytes accessed | tf_op | source)
XLA Modules:
  0.0 30.9 jit_solution(17646002206537368679)
XLA Ops:
  0.7 29.0 %retriever_loss.1 = f32[1,128]{1,0:T(1,128)} custom-call(bf16[1,128,1024]{2,1,0:T(8,128)(2,1)} %q_ref.1, bf16[1,256,1024]{2,1,0:T(8,128)(2,1)} %p_ref.1, bf16[256,1024]{1,0:T(8,128)(2,1)} %w_ref.1, s32[1,128]{1,0:T(1,128)} %pos_ref.1, s32[1,1,2]{2,1,0:T(1,128)} %ids_ref.1, s32[1,1]{1,0:T(1,128)S(6)} %copy.8.count_ref), custom_call_target="tpu_custom_call" | custom-call | tf_op jit(solution)/shard_map/retriever_loss/pallas_call | solution.py:369
  29.7 1.2 %copy.9 = f32[1,128]{1,0:T(1,128)} copy(f32[1,128]{1,0:T(1,128)} %retriever_loss.1) | data formatting | bytes 1024
